TPU v7x, 128 devices: a whole 4x4x4 slice. The times are simulated.
128 devices in a mesh: row: 16 (over x, z), col: 8 (over y, core).
Axes of the slice: x: 4, y: 4, z: 4, core: 2. Of those that a mesh axis runs over, the one named last changes fastest.
Arguments:
- root_inverse: float32 [2, 2048, 4, 1024], P(None, 'row', None, 'col'), as said below
- child_coupling: float32 [2, 2, 2048, 2, 1024], P(None, None, 'row', None, 'col'), may hold values from -0.046875 to 0.046875
- child_inverse: float32 [2, 1, 2048, 2, 1024], P(None, None, 'row', None, 'col'), as said below
- pattern: int32 [2, 32], replicated, may hold values 0 or 1
Outputs:
- sigma_root: float32 [2, 2048, 4, 1024], P(None, 'row', None, 'col')
- sigma_coupling: float32 [2, 2, 2048, 2, 1024], P(None, None, 'row', None, 'col')
- sigma_child: float32 [2, 128, 2, 1024], P(None, None, None, 'col')
Inputs may be any that keep to these rules, and one draw needn't show every extreme that they name: `root_inverse`: read row-major as a 4096 x 4096 matrix it is lower triangular with a positive diagonal. `child_inverse`: read row-major each child's 2048 x 2048 matrix is lower triangular with a positive diagonal. `pattern`: 1 where child j's separator couples to root supernode i, else 0.
All inputs are finite; a program needn't handle non-finite values.
Results may differ from a plain program's by a relative error of at most 0.00013.
Values sent between devices are 32-bit elements; how exact they have to be, the bound alone decides.
No kernel may reach another device: no remote copies, remote signals or barrier semaphores. Data moves between devices by JAX's collectives and lax.ppermute only.
A program may use at most 128 MiB of HBM per device.

v0:
```python
import jax
import jax.numpy as jnp
from jax import lax
from jax.sharding import PartitionSpec as P

B = 128
NR = 4096
NC = 2048


def spread(value, axis, source):
    kept = jnp.where(lax.axis_index(axis) == source, value, 0).astype(value.dtype)
    return lax.psum(kept, axis)


def local(root_inverse, child_coupling, child_inverse, pattern):
    highest = lax.Precision.HIGHEST
    rows_axis = lax.axis_size("row")
    cols_axis = lax.axis_size("col")
    my_row = lax.axis_index("row")
    root_blocks, width, col_blocks, _ = root_inverse.shape
    child_count = child_coupling.shape[0]
    child_columns = child_coupling.shape[3]
    local_rows = root_blocks * width
    block_ids = jnp.arange(root_blocks, dtype=jnp.int32) * rows_axis + my_row
    matches = (jnp.arange(NR // B, dtype=jnp.int32)[None, :] == block_ids[:, None]).astype(
        jnp.float32
    )
    keep = jnp.einsum("jn,an->ja", pattern.astype(jnp.float32), matches)
    coupled = child_coupling * keep[:, :, None, None, None]
    root_panel, child_panel = (
        lax.all_gather(root_inverse, "row", axis=1, tiled=True),
        lax.all_gather(child_inverse, "row", axis=2, tiled=True),
    )
    columns = root_panel.reshape(NR, col_blocks * width)
    groups = rows_axis // cols_axis
    chosen = lax.dynamic_index_in_dim(
        columns.reshape(NR, root_blocks, groups, width), my_row // cols_axis, 2, False
    )
    mirrored = spread(chosen.reshape(NR, local_rows), "col", my_row % cols_axis)
    sigma_local = jnp.einsum("km,kn->mn", mirrored, columns, precision=highest)
    sigma_root = sigma_local.reshape(root_blocks, width, col_blocks, width)
    sigma_rows, coupling_rows = (
        lax.all_gather(sigma_root, "col", axis=3, tiled=True),
        lax.all_gather(coupled, "col", axis=4, tiled=True),
    )
    coupling_panel = coupling_rows.reshape(child_count, local_rows, NC)
    inverse_columns = child_panel.reshape(child_count, NC, child_columns * width)
    update = jnp.einsum("jmk,jkn->jmn", coupling_panel, inverse_columns, precision=highest)
    sigma_split = sigma_rows.reshape(local_rows, root_blocks, rows_axis * width)
    update_split = update.reshape(child_count, root_blocks, width, child_columns * width)
    product = jnp.einsum(
        "mak,jakn->jmn",
        sigma_split,
        lax.all_gather(update_split, "row", axis=2, tiled=True),
        precision=highest,
    )
    coupling_sigma = -(
        product.reshape(child_count, root_blocks, width, child_columns * width)
        * keep[:, :, None, None]
    )
    local_inverse = child_inverse.reshape(child_count, -1, child_columns, width)
    first_part = jnp.einsum("jkcr,jkcs->jcrs", local_inverse, local_inverse, precision=highest)
    update_blocks = update.reshape(child_count, local_rows, child_columns, width)
    sigma_blocks = coupling_sigma.reshape(child_count, local_rows, child_columns, width)
    second_part = jnp.einsum("jkcr,jkcs->jcrs", update_blocks, sigma_blocks, precision=highest)
    summed = lax.psum(first_part - second_part, "row")
    sigma_child = summed.transpose(0, 2, 1, 3)
    return (
        sigma_root,
        coupling_sigma.reshape(child_count, root_blocks, width, child_columns, width),
        sigma_child,
    )


def solution(mesh):
    in_specs = (
        P(None, "row", None, "col"),
        P(None, None, "row", None, "col"),
        P(None, None, "row", None, "col"),
        P(),
    )
    out_specs = (
        P(None, "row", None, "col"),
        P(None, None, "row", None, "col"),
        P(None, None, None, "col"),
    )
    return jax.shard_map(local, mesh=mesh, in_specs=in_specs, out_specs=out_specs, check_vma=False)
```

profile of v0, /device:TPU:0, one launch (start us, length us, event | category | flops | bytes accessed | tf_op | source)
XLA Modules:
  0.0 490.8 jit_solution(11845554919135694700)
XLA Ops:
  7.2 0.7 all-gather.6.cloned.1.call-update
  8.0 75.6 %all-gather.6.cloned.1.call-done = f32[2,2048,4,128]{3,2,1,0:T(4,128)} async-done(((f32[2,128,4,128]{3,2,1,0:T(4,128)}), f32[2,2048,4,128]{3,2,1,0:T(4,128)}) %all-gather.6.cloned.1.call-update) | async-done | bytes 8388624 | tf_op jit(solution)/shard_map/all_gather | solution.py:32
  83.6 7.3 %broadcast_select_fusion = f32[4096,2,1,128]{3,2,1,0:T(1,128)} fusion(pred[]{:T(512)S(6)} %eq.18, f32[4096,2,2,128]{3,2,1,0:T(2,128)} %bitcast.53, s32[]{:T(128)S(6)} %select_n.29), kind=kLoop, calls=%fused_computation.1 | loop fusion | flops 1048576 | bytes 8388613 | tf_op jit(solution)/shard_map/jit(_where)/select_n | solution.py:12
  90.8 10.2 %copy.19 = f32[4096,2,1,128]{0,3,1,2:T(8,128)} copy(f32[4096,2,1,128]{3,2,1,0:T(1,128)} %broadcast_select_fusion) | data formatting | bytes 8388608 | tf_op jit(solution)/shard_map/jit(_where)/select_n | solution.py:12
  101.1 0.6 copy-done.3
  102.1 1.0 broadcast_multiply_fusion
  103.2 0.5 all-gather.10.cloned.1.call-update
  103.7 7.6 %copy.44 = f32[512,8,4,128]{3,1,2,0:T(8,128)} copy(f32[512,8,4,128]{3,2,1,0:T(4,128)} %bitcast.54) | data formatting | bytes 16777216
  111.3 9.0 %copy.20 = f32[4096,512]{0,1:T(8,128)} copy(f32[4096,512]{1,0:T(8,128)} %bitcast.52) | data formatting | bytes 16777216 | tf_op jit(solution)/shard_map/reshape | solution.py:35
  120.3 53.0 %all-reduce.3.cloned.1.call-done = f32[2,128,4096]{2,1,0:T(8,128)} async-done(((f32[2,128,4096]{2,1,0:T(8,128)}), f32[2,128,4096]{2,1,0:T(8,128)}) %all-reduce.3.cloned.1.call-update) | async-done | bytes 4194320 | tf_op jit(solution)/shard_map/psum | solution.py:13
  173.3 11.0 %fusion = f32[2,128,4,128]{3,1,2,0:T(8,128)} fusion(f32[4,128,4096,1]{2,1,0,3:T(8,128)} %bitcast.51, f32[2,128,4096]{2,1,0:T(8,128)} %all-reduce.3.cloned.1.call-done), kind=kOutput, calls=%fused_computation.2 | convolution fusion | flops 6442450944 | bytes 13107200 | tf_op jit(solution)/shard_map/km,kn->mn/dot_general | solution.py:41
  184.4 27.3 %all-gather.8.cloned.1.call-done = f32[2,2,128,2,1024]{4,3,2,1,0:T(2,128)} async-done(((f32[2,2,128,2,128]{4,3,2,1,0:T(2,128)}), f32[2,2,128,2,1024]{4,3,2,1,0:T(2,128)}) %all-gather.8.cloned.1.call-update) | async-done | bytes 4194320 | tf_op jit(solution)/shard_map/all_gather | solution.py:45
  211.7 6.6 %reshape.53 = f32[2,256,2048]{2,1,0:T(8,128)} reshape(f32[2,2,128,2,1024]{4,3,2,1,0:T(2,128)} %all-gather.8.cloned.1.call-done) | data formatting | bytes 8388608 | tf_op jit(solution)/shard_map/reshape | solution.py:47
  218.3 48.1 %all-gather.10.cloned.1.call-done = f32[2,1,2048,2,128]{4,3,2,1,0:T(2,128)} async-done(((f32[2,1,128,2,128]{4,3,2,1,0:T(2,128)}), f32[2,1,2048,2,128]{4,3,2,1,0:T(2,128)}) %all-gather.10.cloned.1.call-update) | async-done | bytes 4194320 | tf_op jit(solution)/shard_map/all_gather | solution.py:33
  266.4 6.4 %reshape.54 = f32[2,2048,256]{2,1,0:T(8,128)} reshape(f32[2,1,2048,2,128]{4,3,2,1,0:T(2,128)} %all-gather.10.cloned.1.call-done) | data formatting | bytes 8388608 | tf_op jit(solution)/shard_map/reshape | solution.py:48
  272.9 8.1 %fusion.14 = f32[2,256,256]{2,1,0:T(8,128)S(1)} fusion(f32[2,256,2048]{2,1,0:T(8,128)} %reshape.53, f32[2,2048,256]{2,1,0:T(8,128)} %reshape.54), kind=kOutput, calls=%fused_computation.23 | convolution fusion | flops 3221225472 | bytes 8912896 | tf_op jit(solution)/shard_map/jmk,jkn->jmn/dot_general | solution.py:49
  280.9 1.0 copy.22
  282.0 0.2 all-reduce.5.cloned.1.call-start
  282.3 0.2 copy.37
  282.5 21.7 %all-gather.14.cloned.1.call-done = f32[2,128,4,1024]{3,1,2,0:T(8,128)} async-done(((f32[2,128,4,128]{3,1,2,0:T(8,128)}), f32[2,128,4,1024]{3,1,2,0:T(8,128)}) %all-gather.14.cloned.1.call-update) | async-done | bytes 4194320 | tf_op jit(solution)/shard_map/all_gather | solution.py:44
  304.2 7.3 %copy.23 = f32[2,128,4,1024]{1,0,3,2:T(2,128)} copy(f32[2,128,4,1024]{3,1,2,0:T(8,128)} %all-gather.14.cloned.1.call-done) | data formatting | bytes 8388608 | tf_op jit(solution)/shard_map/all_gather | solution.py:44
  311.5 6.4 %reshape.56 = f32[256,2,2048]{0,2,1:T(8,128)} reshape(f32[2,128,4,1024]{1,0,3,2:T(2,128)} %copy.23) | data formatting | bytes 8388608 | tf_op jit(solution)/shard_map/reshape | solution.py:50
  317.9 68.3 %all-gather.12.cloned.1.call-done = f32[2,2,2048,256]{2,3,1,0:T(8,128)} async-done(((f32[2,2,128,256]{2,3,1,0:T(8,128)}), f32[2,2,2048,256]{2,3,1,0:T(8,128)}) %all-gather.12.cloned.1.call-update) | async-done | bytes 8388624 | tf_op jit(solution)/shard_map/all_gather | solution.py:55
  386.2 9.8 %fusion.2 = f32[2,256,256,1]{2,1,3,0:T(8,128)S(1)} fusion(f32[2,2,2048,256]{2,3,1,0:T(8,128)} %all-gather.12.cloned.1.call-done, f32[256,2,2048]{0,2,1:T(8,128)} %reshape.56), kind=kOutput, calls=%fused_computation.4 | convolution fusion | flops 6442450944 | bytes 13107200 | tf_op jit(solution)/shard_map/mak,jakn->jmn/dot_general | solution.py:52
  396.2 0.8 fusion.5
  397.0 1.3 fusion.4
  398.3 1.1 copy.31
  399.5 0.3 reshape.57
  399.7 0.4 copy.25
  400.2 1.1 multiply_negate_fusion
  401.2 80.9 %all-reduce.5.cloned.1.call-done = f32[2,128,2,128]{3,1,2,0:T(8,128)} async-done(((f32[2,128,2,128]{3,1,2,0:T(8,128)}), f32[2,128,2,128]{3,1,2,0:T(8,128)}) %all-reduce.5.cloned.1.call-update) | async-done | bytes 262160 | tf_op jit(solution)/shard_map/psum | solution.py:67
  482.1 1.9 copy.32
  (24 shorter events, 1.0 us)
Async XLA Ops:
  7.2 76.4 %all-gather.6.cloned.1.call-start = ((), (), s32[]{:S(2)}) async-start(), calls=%async_computation | async-start | bytes 8912896 | tf_op jit(solution)/shard_map/all_gather | solution.py:32
  7.9 165.4 %all-reduce.3.cloned.1.call-start = ((), (), s32[]{:S(2)}) async-start(), calls=%async_computation.1 | async-start | bytes 8388608 | tf_op jit(solution)/shard_map/psum | solution.py:13
  101.0 0.7 copy-start.3
  101.0 1.1 copy-start.2
  101.0 110.6 %all-gather.8.cloned.1.call-start = ((), (), s32[]{:S(2)}) async-start(), calls=%async_computation.2 | async-start | bytes 4718592 | tf_op jit(solution)/shard_map/all_gather | solution.py:45
  103.1 163.3 %all-gather.10.cloned.1.call-start = ((), (), s32[]{:S(2)}) async-start(), calls=%async_computation.3 | async-start | bytes 4456448 | tf_op jit(solution)/shard_map/all_gather | solution.py:33
  103.7 200.5 %all-gather.14.cloned.1.call-start = ((), (), s32[]{:S(2)}) async-start(), calls=%async_computation.5 | async-start | bytes 4718592 | tf_op jit(solution)/shard_map/all_gather | solution.py:44
  184.3 201.9 %all-gather.12.cloned.1.call-start = ((), (), s32[]{:S(2)}) async-start(), calls=%async_computation.4 | async-start | bytes 8912896 | tf_op jit(solution)/shard_map/all_gather | solution.py:55
  282.0 200.1 %all-reduce.5.cloned.1.call-start = ((), (), s32[]{:S(2)}) async-start(), calls=%async_computation.6 | async-start | bytes 524288 | tf_op jit(solution)/shard_map/psum | solution.py:67
  317.9 79.1 %copy-start.1 = (f32[2,1,128,2,128]{4,3,2,1,0:T(2,128)S(1)}, f32[2,1,128,2,128]{4,3,2,1,0:T(2,128)}, u32[]{:S(2)}) copy-start(f32[2,1,128,2,128]{4,3,2,1,0:T(2,128)} %param.6) | copy-start | bytes 786436
  317.9 80.4 %copy-start = (f32[2,128,4,128]{3,1,2,0:T(8,128)S(1)}, f32[2,128,4,128]{3,1,2,0:T(8,128)}, u32[]{:S(2)}) copy-start(f32[2,128,4,128]{3,1,2,0:T(8,128)} %fusion) | copy-start | bytes 1572868
Sparse Core Ops, SparseCore 0:
  10.2 73.3 all-gather.5
  101.1 72.0 all-reduce.2
  175.5 36.0 all-gather.7
  213.7 52.6 all-gather.9
  268.5 35.6 all-gather.13
  306.7 79.4 all-gather.11
  398.4 83.6 all-reduce.4
where the time goes:
time: 492 us; the launch traced here: 491 us
  waiting for transfers between devices  376 us (76%)
  local copies, waits for them, and re-layouts  59.4 us (12%)
  matrix products  31.1 us (6%)
  between operations  14.2 us (3%)
  other arithmetic  9.37 us (2%)
    psum x1, waiting for transfers between devices, local(): summed = lax.psum(first_part - second_part, 'row')  80.9 us
    all_gather x1, waiting for transfers between devices, local(): lax.all_gather(root_inverse, 'row', axis=1, tiled=True)  75.6 us
    all_gather x1, waiting for transfers between devices, local(): lax.all_gather(update_split, 'row', axis=2, tiled=True)  68.3 us
    psum x1, waiting for transfers between devices, spread(): return lax.psum(kept, axis)  53 us
    all_gather x1, waiting for transfers between devices, local(): lax.all_gather(child_inverse, 'row', axis=2, tiled=True)  48.1 us
    all_gather x1, waiting for transfers between devices, local(): lax.all_gather(coupled, 'col', axis=4, tiled=True)  27.3 us
    all_gather x1, waiting for transfers between devices, local(): lax.all_gather(sigma_root, 'col', axis=3, tiled=True)  21.7 us
    unnamed x13, local copies, waits for them, and re-layouts  11.4 us
  transfers between devices with their start and end apart: 7, of which 7 were waited for; matrix products, arithmetic and copies ran while one was open for 14% of the time, Pallas kernels for 0%

commit v1 on v0

--- a/solution.py
+++ b/solution.py
@@ -64,7 +64,7 @@
     update_blocks = update.reshape(child_count, local_rows, child_columns, width)
     sigma_blocks = coupling_sigma.reshape(child_count, local_rows, child_columns, width)
     second_part = jnp.einsum("jkcr,jkcs->jcrs", update_blocks, sigma_blocks, precision=highest)
-    summed = lax.psum(first_part - second_part, "row")
+    summed = lax.all_gather(first_part - second_part, "row").sum(axis=0)
     sigma_child = summed.transpose(0, 2, 1, 3)
     return (
         sigma_root,

time: 492 us -> 461 us (0.937)
  waiting for transfers between devices: 376 us -> 343 us
    psum x1 -> x0, waiting for transfers between devices: 80.9 us -> none  [local(): summed = lax.psum(first_part - second_part, 'row')]
    all_gather x0 -> x1, waiting for transfers between devices: none -> 48.2 us  [local(): summed = lax.all_gather(first_part - second_part, 'row').sum(axis=0)]
  transfers between devices with their start and end apart: 7 -> 7, of which waited for: 7 -> 7; matrix products, arithmetic and copies ran while one was open for 14% -> 15% of each run, Pallas kernels for 0% -> 0%
where the time goes in v1:
time: 461 us; the launch traced here: 460 us
  waiting for transfers between devices  343 us (74%)
  local copies, waits for them, and re-layouts  58.5 us (13%)
  matrix products  31.1 us (7%)
  between operations  14.2 us (3%)
  other arithmetic  11.8 us (3%)
    all_gather x1, waiting for transfers between devices, local(): lax.all_gather(root_inverse, 'row', axis=1, tiled=True)  75.6 us
    all_gather x1, waiting for transfers between devices, local(): lax.all_gather(update_split, 'row', axis=2, tiled=True)  68.3 us
    psum x1, waiting for transfers between devices, spread(): return lax.psum(kept, axis)  53 us
    all_gather x1, waiting for transfers between devices, local(): summed = lax.all_gather(first_part - second_part, 'row').sum(axis=0)  48.2 us
    all_gather x1, waiting for transfers between devices, local(): lax.all_gather(child_inverse, 'row', axis=2, tiled=True)  48.1 us
    all_gather x1, waiting for transfers between devices, local(): lax.all_gather(coupled, 'col', axis=4, tiled=True)  27.3 us
    all_gather x1, waiting for transfers between devices, local(): lax.all_gather(sigma_root, 'col', axis=3, tiled=True)  21.7 us
    dot_general x1, matrix products, local(): sigma_local = jnp.einsum('km,kn->mn', mirrored, columns, precision=highest)  11 us
  transfers between devices with their start and end apart: 7, of which 7 were waited for; matrix products, arithmetic and copies ran while one was open for 15% of the time, Pallas kernels for 0%

profile of v1, /device:TPU:0, one launch (start us, length us, event | category | flops | bytes accessed | tf_op | source)
XLA Modules:
  0.0 459.6 jit_solution(628824909064304684)
XLA Ops:
  7.2 0.7 all-gather.8.cloned.1.call-update
  8.0 75.6 %all-gather.8.cloned.1.call-done = f32[2,2048,4,128]{3,2,1,0:T(4,128)} async-done(((f32[2,128,4,128]{3,2,1,0:T(4,128)}), f32[2,2048,4,128]{3,2,1,0:T(4,128)}) %all-gather.8.cloned.1.call-update) | async-done | bytes 8388624 | tf_op jit(solution)/shard_map/all_gather | solution.py:32
  83.6 7.3 %broadcast_select_fusion = f32[4096,2,1,128]{3,2,1,0:T(1,128)} fusion(pred[]{:T(512)S(6)} %eq.18, f32[4096,2,2,128]{3,2,1,0:T(2,128)} %bitcast.53, s32[]{:T(128)S(6)} %select_n.29), kind=kLoop, calls=%fused_computation.1 | loop fusion | flops 1048576 | bytes 8388613 | tf_op jit(solution)/shard_map/jit(_where)/select_n | solution.py:12
  90.8 10.2 %copy.31 = f32[4096,2,1,128]{0,3,1,2:T(8,128)} copy(f32[4096,2,1,128]{3,2,1,0:T(1,128)} %broadcast_select_fusion) | data formatting | bytes 8388608 | tf_op jit(solution)/shard_map/jit(_where)/select_n | solution.py:12
  101.1 0.6 copy-done.3
  102.1 1.0 broadcast_multiply_fusion
  103.2 0.5 all-gather.12.cloned.1.call-update
  103.7 7.6 %copy.56 = f32[512,8,4,128]{3,1,2,0:T(8,128)} copy(f32[512,8,4,128]{3,2,1,0:T(4,128)} %bitcast.54) | data formatting | bytes 16777216
  111.3 9.0 %copy.32 = f32[4096,512]{0,1:T(8,128)} copy(f32[4096,512]{1,0:T(8,128)} %bitcast.52) | data formatting | bytes 16777216 | tf_op jit(solution)/shard_map/reshape | solution.py:35
  120.3 53.0 %all-reduce.2.cloned.1.call-done = f32[2,128,4096]{2,1,0:T(8,128)} async-done(((f32[2,128,4096]{2,1,0:T(8,128)}), f32[2,128,4096]{2,1,0:T(8,128)}) %all-reduce.2.cloned.1.call-update) | async-done | bytes 4194320 | tf_op jit(solution)/shard_map/psum | solution.py:13
  173.3 11.0 %fusion = f32[2,128,4,128]{3,1,2,0:T(8,128)} fusion(f32[4,128,4096,1]{2,1,0,3:T(8,128)} %bitcast.51, f32[2,128,4096]{2,1,0:T(8,128)} %all-reduce.2.cloned.1.call-done), kind=kOutput, calls=%fused_computation.2 | convolution fusion | flops 6442450944 | bytes 13107200 | tf_op jit(solution)/shard_map/km,kn->mn/dot_general | solution.py:41
  184.4 27.3 %all-gather.10.cloned.1.call-done = f32[2,2,128,2,1024]{4,3,2,1,0:T(2,128)} async-done(((f32[2,2,128,2,128]{4,3,2,1,0:T(2,128)}), f32[2,2,128,2,1024]{4,3,2,1,0:T(2,128)}) %all-gather.10.cloned.1.call-update) | async-done | bytes 4194320 | tf_op jit(solution)/shard_map/all_gather | solution.py:45
  211.7 6.6 %reshape.53 = f32[2,256,2048]{2,1,0:T(8,128)} reshape(f32[2,2,128,2,1024]{4,3,2,1,0:T(2,128)} %all-gather.10.cloned.1.call-done) | data formatting | bytes 8388608 | tf_op jit(solution)/shard_map/reshape | solution.py:47
  218.3 48.1 %all-gather.12.cloned.1.call-done = f32[2,1,2048,2,128]{4,3,2,1,0:T(2,128)} async-done(((f32[2,1,128,2,128]{4,3,2,1,0:T(2,128)}), f32[2,1,2048,2,128]{4,3,2,1,0:T(2,128)}) %all-gather.12.cloned.1.call-update) | async-done | bytes 4194320 | tf_op jit(solution)/shard_map/all_gather | solution.py:33
  266.4 6.4 %reshape.54 = f32[2,2048,256]{2,1,0:T(8,128)} reshape(f32[2,1,2048,2,128]{4,3,2,1,0:T(2,128)} %all-gather.12.cloned.1.call-done) | data formatting | bytes 8388608 | tf_op jit(solution)/shard_map/reshape | solution.py:48
  272.9 8.1 %fusion.13 = f32[2,256,256]{2,1,0:T(8,128)S(1)} fusion(f32[2,256,2048]{2,1,0:T(8,128)} %reshape.53, f32[2,2048,256]{2,1,0:T(8,128)} %reshape.54), kind=kOutput, calls=%fused_computation.22 | convolution fusion | flops 3221225472 | bytes 8912896 | tf_op jit(solution)/shard_map/jmk,jkn->jmn/dot_general | solution.py:49
  280.9 1.0 copy.34
  282.0 0.2 all-gather.18.cloned.1.call-start
  282.5 21.7 %all-gather.16.cloned.1.call-done = f32[2,128,4,1024]{3,1,2,0:T(8,128)} async-done(((f32[2,128,4,128]{3,1,2,0:T(8,128)}), f32[2,128,4,1024]{3,1,2,0:T(8,128)}) %all-gather.16.cloned.1.call-update) | async-done | bytes 4194320 | tf_op jit(solution)/shard_map/all_gather | solution.py:44
  304.2 7.3 %copy.35 = f32[2,128,4,1024]{1,0,3,2:T(2,128)} copy(f32[2,128,4,1024]{3,1,2,0:T(8,128)} %all-gather.16.cloned.1.call-done) | data formatting | bytes 8388608 | tf_op jit(solution)/shard_map/all_gather | solution.py:44
  311.5 6.4 %reshape.56 = f32[256,2,2048]{0,2,1:T(8,128)} reshape(f32[2,128,4,1024]{1,0,3,2:T(2,128)} %copy.35) | data formatting | bytes 8388608 | tf_op jit(solution)/shard_map/reshape | solution.py:50
  317.9 68.3 %all-gather.14.cloned.1.call-done = f32[2,2,2048,256]{2,3,1,0:T(8,128)} async-done(((f32[2,2,128,256]{2,3,1,0:T(8,128)}), f32[2,2,2048,256]{2,3,1,0:T(8,128)}) %all-gather.14.cloned.1.call-update) | async-done | bytes 8388624 | tf_op jit(solution)/shard_map/all_gather | solution.py:55
  386.2 9.8 %fusion.2 = f32[2,256,256,1]{2,1,3,0:T(8,128)S(1)} fusion(f32[2,2,2048,256]{2,3,1,0:T(8,128)} %all-gather.14.cloned.1.call-done, f32[256,2,2048]{0,2,1:T(8,128)} %reshape.56), kind=kOutput, calls=%fused_computation.4 | convolution fusion | flops 6442450944 | bytes 13107200 | tf_op jit(solution)/shard_map/mak,jakn->jmn/dot_general | solution.py:52
  396.2 0.8 fusion.4
  397.0 1.3 convolution_subtract_fusion
  398.3 1.1 copy.43
  399.5 0.3 reshape.57
  399.7 0.4 copy.37
  400.2 1.1 multiply_negate_fusion
  401.2 48.2 %all-gather.18.cloned.1.call-done = f32[32,2,128,128]{3,2,1,0:T(8,128)} async-done(((f32[2,2,128,128]{3,2,1,0:T(8,128)}), f32[32,2,128,128]{3,2,1,0:T(8,128)}) %all-gather.18.cloned.1.call-update) | async-done | bytes 4194320 | tf_op jit(solution)/shard_map/all_gather | solution.py:67
  449.4 2.4 reduce_sum.9
  451.8 0.9 copy.44
  (25 shorter events, 1.2 us)
Async XLA Ops:
  7.2 76.4 %all-gather.8.cloned.1.call-start = ((), (), s32[]{:S(2)}) async-start(), calls=%async_computation | async-start | bytes 8912896 | tf_op jit(solution)/shard_map/all_gather | solution.py:32
  7.9 165.4 %all-reduce.2.cloned.1.call-start = ((), (), s32[]{:S(2)}) async-start(), calls=%async_computation.1 | async-start | bytes 8388608 | tf_op jit(solution)/shard_map/psum | solution.py:13
  101.0 0.7 copy-start.3
  101.0 1.1 copy-start.2
  101.0 110.6 %all-gather.10.cloned.1.call-start = ((), (), s32[]{:S(2)}) async-start(), calls=%async_computation.2 | async-start | bytes 4718592 | tf_op jit(solution)/shard_map/all_gather | solution.py:45
  103.1 163.3 %all-gather.12.cloned.1.call-start = ((), (), s32[]{:S(2)}) async-start(), calls=%async_computation.3 | async-start | bytes 4456448 | tf_op jit(solution)/shard_map/all_gather | solution.py:33
  103.7 200.5 %all-gather.16.cloned.1.call-start = ((), (), s32[]{:S(2)}) async-start(), calls=%async_computation.5 | async-start | bytes 4718592 | tf_op jit(solution)/shard_map/all_gather | solution.py:44
  184.3 201.9 %all-gather.14.cloned.1.call-start = ((), (), s32[]{:S(2)}) async-start(), calls=%async_computation.4 | async-start | bytes 8912896 | tf_op jit(solution)/shard_map/all_gather | solution.py:55
  282.0 167.5 %all-gather.18.cloned.1.call-start = ((), (), s32[]{:S(2)}) async-start(), calls=%async_computation.6 | async-start | bytes 4456448 | tf_op jit(solution)/shard_map/all_gather | solution.py:67
  317.9 79.1 %copy-start.1 = (f32[2,1,128,2,128]{4,3,2,1,0:T(2,128)S(1)}, f32[2,1,128,2,128]{4,3,2,1,0:T(2,128)}, u32[]{:S(2)}) copy-start(f32[2,1,128,2,128]{4,3,2,1,0:T(2,128)} %param.6) | copy-start | bytes 786436
  317.9 80.4 %copy-start = (f32[2,128,4,128]{3,1,2,0:T(8,128)S(1)}, f32[2,128,4,128]{3,1,2,0:T(8,128)}, u32[]{:S(2)}) copy-start(f32[2,128,4,128]{3,1,2,0:T(8,128)} %fusion) | copy-start | bytes 1572868
Sparse Core Ops, SparseCore 0:
  10.2 73.3 all-gather.7
  101.1 72.0 all-reduce.1
  175.5 36.0 all-gather.9
  213.7 52.6 all-gather.11
  268.5 35.6 all-gather.15
  306.7 79.4 all-gather.13
  398.4 50.9 all-gather.17
